TPU v7x, 32 devices: a whole 2x2x4 slice. The times are simulated.
32 devices in a mesh: dp: 8 (over z, x), expert: 4 (over y, core).
Axes of the slice: x: 2, y: 2, z: 4, core: 2. Of those that a mesh axis runs over, the one named last changes fastest.
Arguments:
- tokens: bfloat16 [1024, 4096], P('dp', 'expert'), may hold values from -6 to 6
- expert_ids: int32 [1024, 8], P('dp'), may hold values from 0 to 7, all different within a row; in each aligned block of 128 rows (0 to 127, 128 to 255, ...) at most 128 rows name the same one
- scores: float32 [1024, 8], P('dp'), may hold values from 0.05 to 1
- weight_in: bfloat16 [8, 4096, 2048], P('dp', 'expert'), may hold values from -0.09375 to 0.09375
- weight_out: bfloat16 [8, 1024, 4096], P('dp', None, 'expert'), may hold values from -0.1875 to 0.1875
- out_grad: bfloat16 [1024, 4096], P('dp', 'expert'), may hold values from -6 to 6
Outputs:
- layer_out: bfloat16 [1024, 4096], P('dp', 'expert')
- tokens_grad: bfloat16 [1024, 4096], P('dp', 'expert')
- scores_grad: float32 [1024, 8], P('dp')
- w_in_grad: bfloat16 [8, 4096, 2048], P('dp', 'expert')
- w_out_grad: bfloat16 [8, 1024, 4096], P('dp', None, 'expert')
Inputs may be any that keep to these rules, and one draw needn't show every extreme that they name: `expert_ids`: the 8 experts of a token differ. Among the 128 consecutive tokens of one index of dp no expert is named by more than 128 choices, and in every draw some such block names some expert exactly 128 times.
All inputs are finite; a program needn't handle non-finite values.
Results may differ from a plain program's by a relative error of at most 0.0064.
Values may be sent and summed in bfloat16 or wider, within the bound.
A program may use at most 128 MiB of HBM per device.

v0:
```python
import jax
import jax.numpy as jnp
from jax import lax
from jax.sharding import PartitionSpec as P

ROUTE_SCALE = 2.5


def gate_terms(gate_up, hidden_units):
    gate = gate_up[:, :hidden_units]
    upward = gate_up[:, hidden_units:]
    return (gate, upward, jax.nn.sigmoid(gate))


def gate_backward(hidden_grad, gate, upward, sigma):
    return jnp.concatenate(
        [hidden_grad * upward * sigma * (1.0 + gate * (1.0 - sigma)), hidden_grad * gate * sigma],
        axis=1,
    ).astype(jnp.bfloat16)


def body(tokens, expert_ids, scores, weight_in, weight_out, out_grad):
    n_data = lax.axis_size("dp")
    tok_count, slab_width = tokens.shape
    top_count = expert_ids.shape[1]
    hidden_units = weight_out.shape[1]
    capacity = min(tok_count, 5 * tok_count * top_count // (4 * n_data))
    routed = tok_count * top_count
    group_rows = n_data * capacity
    slot_count = n_data * capacity
    flat_ids = expert_ids.reshape(routed)
    expert_hot = (flat_ids[:, None] == jnp.arange(n_data, dtype=jnp.int32)[None, :]).astype(
        jnp.int32
    )
    earlier = jnp.sum((jnp.cumsum(expert_hot, axis=0) - expert_hot) * expert_hot, axis=1)
    target = flat_ids * capacity + earlier
    placing = (jnp.arange(slot_count, dtype=jnp.int32)[:, None] == target[None, :]).astype(
        jnp.bfloat16
    )
    token_place = jnp.sum(
        placing.reshape(slot_count, tok_count, top_count).astype(jnp.float32), axis=2
    ).astype(jnp.bfloat16)
    score_total = jnp.sum(scores, axis=1, keepdims=True)
    route_weights = ROUTE_SCALE * scores / score_total
    routed_grad = (route_weights[:, :, None] * out_grad.astype(jnp.float32)[:, None, :]).astype(
        jnp.bfloat16
    )
    routed_grad = routed_grad.reshape(routed, slab_width)
    token_send = jnp.dot(token_place, tokens, preferred_element_type=jnp.float32).astype(
        jnp.bfloat16
    )
    grad_send = jnp.dot(placing, routed_grad, preferred_element_type=jnp.float32).astype(
        jnp.bfloat16
    )
    token_slab, grad_slab = (
        lax.all_to_all(
            token_send.reshape(n_data, capacity, slab_width),
            "dp",
            split_axis=0,
            concat_axis=0,
            tiled=True,
        ),
        lax.all_to_all(
            grad_send.reshape(n_data, capacity, slab_width),
            "dp",
            split_axis=0,
            concat_axis=0,
            tiled=True,
        ),
    )
    token_slab = token_slab.reshape(group_rows, slab_width)
    grad_slab = grad_slab.reshape(group_rows, slab_width)
    in_slab = weight_in[0]
    out_slab = weight_out[0]
    gate_up_own = lax.psum_scatter(
        jnp.dot(token_slab, in_slab, preferred_element_type=jnp.float32),
        "expert",
        scatter_dimension=0,
        tiled=True,
    )
    gate_own, up_own, sig_own = gate_terms(gate_up_own, hidden_units)
    hidden_own = (gate_own * sig_own * up_own).astype(jnp.bfloat16)
    piece = lax.all_gather(hidden_own, "expert", axis=0, tiled=True)
    product = jnp.dot(piece, out_slab, preferred_element_type=jnp.float32)
    out_rows = product
    weight_sum = jnp.einsum("rf,rd->fd", piece, grad_slab, preferred_element_type=jnp.float32)
    out_rows, out_weight_sum = (out_rows, weight_sum)
    expert_out = out_rows.astype(jnp.bfloat16)
    out_blocks = expert_out.reshape(n_data, capacity, slab_width)
    out_back = lax.all_to_all(out_blocks, "dp", split_axis=0, concat_axis=0, tiled=True)
    hidden_grad = lax.psum_scatter(
        jnp.einsum("rd,fd->rf", grad_slab, out_slab, preferred_element_type=jnp.float32),
        "expert",
        scatter_dimension=0,
        tiled=True,
    )
    gate_up_grad = gate_backward(hidden_grad, gate_own, up_own, sig_own)
    piece = lax.all_gather(gate_up_grad, "expert", axis=0, tiled=True)
    product = jnp.einsum("rh,dh->rd", piece, in_slab, preferred_element_type=jnp.float32)
    input_rows = product
    weight_sum = jnp.einsum("rd,rh->dh", token_slab, piece, preferred_element_type=jnp.float32)
    input_rows, in_weight_sum = (input_rows, weight_sum)
    grad_blocks = input_rows.astype(jnp.bfloat16).reshape(n_data, capacity, slab_width)
    grad_back = lax.all_to_all(grad_blocks, "dp", split_axis=0, concat_axis=0, tiled=True)
    outputs_in = out_back.reshape(slot_count, slab_width)
    grads_in = grad_back.reshape(slot_count, slab_width)
    picked = jnp.einsum("sr,sd->rd", placing, outputs_in, preferred_element_type=jnp.float32)
    picked = picked.reshape(tok_count, top_count, slab_width)
    layer_out = jnp.sum(route_weights[:, :, None] * picked, axis=1).astype(jnp.bfloat16)
    partial_dot = jnp.sum(out_grad.astype(jnp.float32)[:, None, :] * picked, axis=2)
    choice_dot = lax.psum(partial_dot, "expert")
    scores_grad = (
        ROUTE_SCALE * choice_dot - jnp.sum(choice_dot * route_weights, axis=1, keepdims=True)
    ) / score_total
    tokens_grad = jnp.einsum(
        "st,sd->td", token_place, grads_in, preferred_element_type=jnp.float32
    ).astype(jnp.bfloat16)
    return (
        layer_out,
        tokens_grad,
        scores_grad,
        in_weight_sum.astype(jnp.bfloat16)[None],
        out_weight_sum.astype(jnp.bfloat16)[None],
    )


def solution(mesh):
    placed = (
        P("dp", "expert"),
        P("dp", None),
        P("dp", None),
        P("dp", "expert", None),
        P("dp", None, "expert"),
        P("dp", "expert"),
    )
    return jax.shard_map(
        body,
        mesh=mesh,
        in_specs=placed,
        out_specs=(
            P("dp", "expert"),
            P("dp", "expert"),
            P("dp", None),
            P("dp", "expert", None),
            P("dp", None, "expert"),
        ),
        check_vma=False,
    )
```

profile of v0, /device:TPU:0, one launch (start us, length us, event | category | flops | bytes accessed | tf_op | source)
XLA Modules:
  0.0 358.3 jit_solution(17069824510494278459)
XLA Ops:
  7.2 0.9 copy.27
  8.4 2.3 reduce-window.6
  11.2 0.7 reduce_sum.59
  11.9 0.7 multiply_divide_fusion
  12.8 1.0 convert_element_type.56
  13.8 2.4 fusion.22
  16.2 55.3 %all_to_all.20 = bf16[8,128,1024]{2,1,0:T(8,128)(2,1)S(1)} all-to-all(bf16[8,128,1024]{2,1,0:T(8,128)(2,1)S(1)} %bitcast.76), channel_id=1, replica_groups=mesh['dp'=8,'expert'=4] {'dp'}, dimensions={0} | all-to-all | bytes 4194304 | tf_op jit(solution)/shard_map/all_to_all | solution.py:63
  71.5 1.3 copy-done.1
  72.8 4.5 %fusion.13 = f32[1024,1024]{1,0:T(8,128)} fusion(bf16[1024,1024]{1,0:T(8,128)(2,1)S(1)} %bitcast.70, bf16[1,1024,1024]{2,1,0:T(8,128)(2,1)S(1)} %copy-done), kind=kOutput, calls=%fused_computation.19 | convolution fusion | flops 2147483648 | bytes 8388608 | tf_op jit(solution)/shard_map/rd,fd->rf/dot_general | solution.py:92
  78.0 1.9 fusion.10
  79.9 0.7 convolution_convert_fusion
  80.6 51.6 %all_to_all.21 = bf16[8,128,1024]{2,1,0:T(8,128)(2,1)S(1)} all-to-all(bf16[8,128,1024]{2,1,0:T(8,128)(2,1)S(1)} %bitcast.69), channel_id=1, replica_groups=mesh['dp'=8,'expert'=4] {'dp'}, dimensions={0} | all-to-all | bytes 4194304 | tf_op jit(solution)/shard_map/all_to_all | solution.py:56
  132.3 1.4 copy-done.2
  133.6 6.6 %fusion.3 = f32[1024,2048]{1,0:T(8,128)} fusion(bf16[1024,1024]{1,0:T(8,128)(2,1)S(1)} %bitcast.72, bf16[1,1024,2048]{2,1,0:T(8,128)(2,1)S(1)} %copy-done.9), kind=kOutput, calls=%fused_computation.4 | convolution fusion | flops 4294967296 | bytes 14680064 | tf_op jit(solution)/shard_map/dot_general | solution.py:76
  140.4 70.8 %reduce-scatter.3.cloned.1.call-done = f32[256,2048]{1,0:T(8,128)} async-done(((f32[1024,2048]{1,0:T(8,128)}), f32[256,2048]{1,0:T(8,128)}) %reduce-scatter.3.cloned.1.call-update) | async-done | bytes 2097168 | tf_op jit(solution)/shard_map/reduce_scatter | solution.py:75
  211.1 3.4 multiply_convert_fusion.1
  214.8 1.1 pad_maximum_fusion
  215.8 21.4 %all-gather.3.cloned.1.call-done = bf16[1024,1024]{1,0:T(8,128)(2,1)} async-done(((bf16[256,1024]{1,0:T(8,128)(2,1)}), bf16[1024,1024]{1,0:T(8,128)(2,1)}) %all-gather.3.cloned.1.call-update) | async-done | bytes 2097168 | tf_op jit(solution)/shard_map/all_gather | solution.py:83
  237.3 5.2 %fusion.19 = bf16[1024,1024]{1,0:T(8,128)(2,1)} fusion(bf16[1024,1024]{1,0:T(8,128)(2,1)} %all-gather.3.cloned.1.call-done, bf16[1,1024,1024]{2,1,0:T(8,128)(2,1)S(1)} %copy-done), kind=kOutput, calls=%fused_computation.26 | convolution fusion | flops 2148532224 | bytes 6291456 | tf_op jit(solution)/shard_map/dot_general | solution.py:84
  242.5 5.5 %all-to-all-start.1 = ((bf16[8,128,1024]{2,1,0:T(8,128)(2,1)}), bf16[8,128,1024]{2,1,0:T(8,128)(2,1)}, u32[]{:S(2)}, u32[]{:S(2)}) async-start(bf16[8,128,1024]{2,1,0:T(8,128)(2,1)} %bitcast.75), calls=%async_computation.2 | async-start | bytes 4194304 | tf_op jit(solution)/shard_map/all_to_all | solution.py:90
  248.0 25.8 %all-gather.5.cloned.1.call-done = bf16[1024,2048]{1,0:T(8,128)(2,1)} async-done(((bf16[256,2048]{1,0:T(8,128)(2,1)}), bf16[1024,2048]{1,0:T(8,128)(2,1)}) %all-gather.5.cloned.1.call-update) | async-done | bytes 4194320 | tf_op jit(solution)/shard_map/all_gather | solution.py:98
  273.8 9.3 %fusion.25 = bf16[1024,1024]{1,0:T(8,128)(2,1)} fusion(bf16[1024,2048]{1,0:T(8,128)(2,1)} %all-gather.5.cloned.1.call-done, bf16[1,1024,2048]{2,1,0:T(8,128)(2,1)} %param.9), kind=kOutput, calls=%fused_computation.28 | convolution fusion | flops 4296015872 | bytes 10485760 | tf_op jit(solution)/shard_map/rh,dh->rd/dot_general | solution.py:99
  283.1 13.6 %all-to-all-done.1 = bf16[8,128,1024]{2,1,0:T(8,128)(2,1)} async-done(((bf16[8,128,1024]{2,1,0:T(8,128)(2,1)}), bf16[8,128,1024]{2,1,0:T(8,128)(2,1)}, u32[]{:S(2)}, u32[]{:S(2)}) %all-to-all-start.1) | async-done | bytes 2097184 | tf_op jit(solution)/shard_map/all_to_all | solution.py:90
  296.8 4.6 %all-to-all-start.3 = ((bf16[8,128,1024]{2,1,0:T(8,128)(2,1)}), bf16[8,128,1024]{2,1,0:T(8,128)(2,1)}, u32[]{:S(2)}, u32[]{:S(2)}) async-start(bf16[8,128,1024]{2,1,0:T(8,128)(2,1)} %bitcast.74), calls=%async_computation.5 | async-start | bytes 4194304 | tf_op jit(solution)/shard_map/all_to_all | solution.py:104
  301.4 0.7 fusion.5
  302.0 6.1 %convert_bitcast_fusion.1 = bf16[1,1024,1024]{2,1,0:T(8,128)(2,1)} fusion(bf16[1024,1024]{1,0:T(8,128)(2,1)} %all-gather.3.cloned.1.call-done, bf16[1024,1024]{1,0:T(8,128)(2,1)} %bitcast.71), kind=kOutput, calls=%fused_computation.23 | convolution fusion | flops 2148532224 | bytes 6291456 | tf_op jit(solution)/shard_map/rf,rd->fd/dot_general | solution.py:86
  308.1 6.2 %convert_bitcast_fusion = bf16[1,1024,2048]{2,1,0:T(8,128)(2,1)} fusion(bf16[1024,1024]{1,0:T(8,128)(2,1)S(1)} %bitcast.73, bf16[1024,2048]{1,0:T(8,128)(2,1)S(1)} %copy-done.10), kind=kOutput, calls=%fused_computation.6 | convolution fusion | flops 4297064448 | bytes 10485760 | tf_op jit(solution)/shard_map/rd,rh->dh/dot_general | solution.py:101
  314.4 5.2 %multiply_reduce_fusion = (f32[128,8]{0,1:T(8,128)S(1)}, bf16[128,1024]{1,0:T(8,128)(2,1)}) fusion(f32[128,1024]{1,0:T(8,128)S(1)} %copy-done.5, f32[128,8]{0,1:T(8,128)S(1)} %multiply_divide_fusion, bf16[1024,1024,1]{1,0,2:T(8,128)(2,1)} %bitcast.8, pred[128,8,1024]{2,1,0:T(8,128)(4,1)S(1)} %fusion.5), kind=kOutput, calls=%fused_computation.7 | convolution fusion | flops 2151545856 | bytes 3940352 | tf_op jit(solution)/shard_map/sr,sd->rd/dot_general | solution.py:107
  319.5 6.0 %psum.7 = f32[128,8]{0,1:T(8,128)S(1)} all-reduce(f32[128,8]{0,1:T(8,128)S(1)} %get-tuple-element.5), channel_id=1, replica_groups=mesh['dp'=8,'expert'=4] {'expert'}, use_global_device_ids=true, to_apply=%region_9.10 | all-reduce | flops 1024 | bytes 8192 | tf_op jit(solution)/shard_map/psum | solution.py:111
  325.6 0.6 subtract_divide_fusion
  326.2 22.8 %all-to-all-done.3 = bf16[8,128,1024]{2,1,0:T(8,128)(2,1)} async-done(((bf16[8,128,1024]{2,1,0:T(8,128)(2,1)}), bf16[8,128,1024]{2,1,0:T(8,128)(2,1)}, u32[]{:S(2)}, u32[]{:S(2)}) %all-to-all-start.3) | async-done | bytes 2097184 | tf_op jit(solution)/shard_map/all_to_all | solution.py:104
  349.0 2.8 convolution_convert_fusion.1
  (43 shorter events, 2.0 us)
Async XLA Ops:
  7.2 65.7 %copy-start = (bf16[1,1024,1024]{2,1,0:T(8,128)(2,1)S(1)}, bf16[1,1024,1024]{2,1,0:T(8,128)(2,1)}, u32[]{:S(2)}) copy-start(bf16[1,1024,1024]{2,1,0:T(8,128)(2,1)} %param.10) | copy-start | bytes 6291460
  7.2 133.2 %reduce-scatter.5.cloned.1.call-start = ((), (), s32[]{:S(2)}) async-start(), calls=%async_computation.8 | async-start | bytes 5242880 | tf_op jit(solution)/shard_map/reduce_scatter | solution.py:91
  13.8 2.4 copy-start.4
  71.5 1.3 copy-start.1
  77.3 0.7 copy-start.8
  77.3 2.6 copy-start.6
  77.3 133.8 %reduce-scatter.3.cloned.1.call-start = ((), (), s32[]{:S(2)}) async-start(), calls=%async_computation.6 | async-start | bytes 10485760 | tf_op jit(solution)/shard_map/reduce_scatter | solution.py:75
  80.6 53.0 %copy-start.9 = (bf16[1,1024,2048]{2,1,0:T(8,128)(2,1)S(1)}, bf16[1,1024,2048]{2,1,0:T(8,128)(2,1)}, u32[]{:S(2)}) copy-start(bf16[1,1024,2048]{2,1,0:T(8,128)(2,1)} %param.9) | copy-start | bytes 12582916
  132.3 1.4 copy-start.2
  140.3 97.0 %all-gather.3.cloned.1.call-start = ((), (), s32[]{:S(2)}) async-start(), calls=%async_computation.7 | async-start | bytes 2621440 | tf_op jit(solution)/shard_map/all_gather | solution.py:83
  214.5 59.3 %all-gather.5.cloned.1.call-start = ((), (), s32[]{:S(2)}) async-start(), calls=%async_computation.9 | async-start | bytes 5242880 | tf_op jit(solution)/shard_map/all_gather | solution.py:98
  242.5 54.3 %all-to-all-start.1 = ((bf16[8,128,1024]{2,1,0:T(8,128)(2,1)}), bf16[8,128,1024]{2,1,0:T(8,128)(2,1)}, u32[]{:S(2)}, u32[]{:S(2)}) async-start(bf16[8,128,1024]{2,1,0:T(8,128)(2,1)} %bitcast.75), calls=%async_computation.2 | async-start | bytes 4194304 | tf_op jit(solution)/shard_map/all_to_all | solution.py:90
  296.8 52.2 %all-to-all-start.3 = ((bf16[8,128,1024]{2,1,0:T(8,128)(2,1)}), bf16[8,128,1024]{2,1,0:T(8,128)(2,1)}, u32[]{:S(2)}, u32[]{:S(2)}) async-start(bf16[8,128,1024]{2,1,0:T(8,128)(2,1)} %bitcast.74), calls=%async_computation.5 | async-start | bytes 4194304 | tf_op jit(solution)/shard_map/all_to_all | solution.py:104
  302.0 6.1 %copy-start.3 = (bf16[8,128,1024]{2,1,0:T(8,128)(2,1)S(1)}, bf16[8,128,1024]{2,1,0:T(8,128)(2,1)}, u32[]{:S(2)}) copy-start(bf16[8,128,1024]{2,1,0:T(8,128)(2,1)} %copy-done.2) | copy-start | bytes 6291460
  302.0 6.1 %copy-start.10 = (bf16[1024,2048]{1,0:T(8,128)(2,1)S(1)}, bf16[1024,2048]{1,0:T(8,128)(2,1)}, u32[]{:S(2)}) copy-start(bf16[1024,2048]{1,0:T(8,128)(2,1)} %all-gather.5.cloned.1.call-done) | copy-start | bytes 12582916
  308.1 6.2 %copy-start.5 = (f32[128,1024]{1,0:T(8,128)S(1)}, f32[128,1024]{1,0:T(8,128)}, u32[]{:S(2)}) copy-start(f32[128,1024]{1,0:T(8,128)} %copy-done.4) | copy-start | bytes 1572868
  314.4 11.2 %copy-start.7 = (f32[128,8]{0,1:T(8,128)S(1)}, f32[128,8]{0,1:T(8,128)}, u32[]{:S(2)}) copy-start(f32[128,8]{0,1:T(8,128)} %param.8) | copy-start | bytes 12292
Sparse Core Ops, SparseCore 0:
  77.4 43.5 reduce-scatter.4
  140.4 70.6 reduce-scatter.2
  214.6 22.5 all-gather.2
  239.3 34.4 all-gather.4
where the time goes:
time: 359 us; the launch traced here: 358 us
  waiting for transfers between devices  154 us (43%)
  blocking collectives  113 us (31%)
  matrix products  49 us (14%)
  between operations  13.9 us (4%)
  other arithmetic  12.6 us (4%)
  starting transfers between devices  10.4 us (3%)
  local copies, waits for them, and re-layouts  4.91 us (1%)
    reduce_scatter x1, waiting for transfers between devices, body(): lax.psum_scatter(jnp.dot(token_slab, in_slab, preferred_element_type=jnp....  70.8 us
    all_to_all x1, blocking collectives, body(): lax.all_to_all(grad_send.reshape(n_data, capacity, slab_width), 'dp', spl...  55.3 us
    all_to_all x1, blocking collectives, body(): lax.all_to_all(token_send.reshape(n_data, capacity, slab_width), 'dp', sp...  51.6 us
    all_gather x1, waiting for transfers between devices, body(): piece = lax.all_gather(gate_up_grad, 'expert', axis=0, tiled=True)  25.8 us
    all_to_all x1, waiting for transfers between devices, body(): lax.all_to_all(grad_blocks, 'dp', split_axis=0, concat_axis=0, tiled=True)  22.8 us
    all_gather x1, waiting for transfers between devices, body(): piece = lax.all_gather(hidden_own, 'expert', axis=0, tiled=True)  21.4 us
    all_to_all x1, waiting for transfers between devices, body(): lax.all_to_all(out_blocks, 'dp', split_axis=0, concat_axis=0, tiled=True)  13.6 us
    dot_general x1, matrix products, body(): jnp.einsum('rh,dh->rd', piece, in_slab, preferred_element_type=jnp.float32)  9.35 us
  transfers between devices with their start and end apart: 6, of which 5 were waited for; matrix products, arithmetic and copies ran while one was open for 12% of the time, Pallas kernels for 0%

commit v1 on v0

--- a/solution.py
+++ b/solution.py
@@ -19,7 +19,7 @@
     ).astype(jnp.bfloat16)
 
 
-def body(tokens, expert_ids, scores, weight_in, weight_out, out_grad):
+def routed_body(tokens, expert_ids, scores, weight_in, weight_out, out_grad):
     n_data = lax.axis_size("dp")
     tok_count, slab_width = tokens.shape
     top_count = expert_ids.shape[1]
@@ -32,7 +32,13 @@
     expert_hot = (flat_ids[:, None] == jnp.arange(n_data, dtype=jnp.int32)[None, :]).astype(
         jnp.int32
     )
-    earlier = jnp.sum((jnp.cumsum(expert_hot, axis=0) - expert_hot) * expert_hot, axis=1)
+    place = jnp.arange(routed, dtype=jnp.int32)
+    before = jnp.dot(
+        (place[:, None] > place[None, :]).astype(jnp.bfloat16),
+        expert_hot.astype(jnp.bfloat16),
+        preferred_element_type=jnp.float32,
+    ).astype(jnp.int32)
+    earlier = jnp.sum(before * expert_hot, axis=1)
     target = flat_ids * capacity + earlier
     placing = (jnp.arange(slot_count, dtype=jnp.int32)[:, None] == target[None, :]).astype(
         jnp.bfloat16
@@ -124,6 +130,125 @@
     )
 
 
+def swap(value, axis, bit):
+    size = lax.axis_size(axis)
+    return lax.ppermute(value, axis, [(i, i ^ bit) for i in range(size)])
+
+
+def gather_line(block):
+    size = lax.axis_size("dp")
+    line = size // 2
+    ahead, behind = [block], [block]
+    for _ in range(line - 1):
+        ahead.append(lax.ppermute(ahead[-1], "dp", [(i, i + 2) for i in range(size - 2)]))
+        behind.append(lax.ppermute(behind[-1], "dp", [(i, i - 2) for i in range(2, size)]))
+    near = [block] + [ahead[s] + behind[line - s] for s in range(1, line)]
+    near = jnp.concatenate(near, axis=0)
+    return jnp.concatenate([near, swap(near, "dp", 1)], axis=0)
+
+
+def sum_parts(partial, high, low):
+    rows, width = partial.shape
+    quarters = partial.reshape(2, 2, rows // 4, width)
+    kept = jnp.where(low == 0, quarters[:, 0], quarters[:, 1])
+    given = jnp.where(low == 0, quarters[:, 1], quarters[:, 0])
+    pair = kept + swap(given, "expert", 1)
+    away = jnp.where(high == 0, pair[1], pair[0]).astype(jnp.bfloat16)
+    home = jnp.where(high == 0, pair[0], pair[1])
+    return home + swap(away, "expert", 2).astype(jnp.float32)
+
+
+def join_parts(own, high, low):
+    far = swap(own, "expert", 2)
+    pair = jnp.stack([jnp.where(high == 0, own, far), jnp.where(high == 0, far, own)])
+    other = swap(pair, "expert", 1)
+    both = jnp.stack(
+        [jnp.where(low == 0, pair, other), jnp.where(low == 0, other, pair)], axis=1
+    )
+    return both.reshape(4 * own.shape[0], own.shape[1])
+
+
+def from_offsets(blocks):
+    size = lax.axis_size("dp")
+    line = size // 2
+    arrived = [blocks[0]]
+    for r in range(1, size):
+        across, step = r // line, r % line
+        pairs = [(i, ((i // 2 - step) % line) * 2 + ((i % 2) ^ across)) for i in range(size)]
+        arrived.append(lax.ppermute(blocks[r], "dp", pairs))
+    return arrived
+
+
+def send_home(blocks):
+    total = blocks[0].astype(jnp.float32)
+    for arrived in from_offsets(blocks)[1:]:
+        total = total + arrived.astype(jnp.float32)
+    return total.astype(jnp.bfloat16)
+
+
+def dense_body(tokens, expert_ids, scores, weight_in, weight_out, out_grad):
+    n_data = lax.axis_size("dp")
+    line = n_data // 2
+    tok_count, slab_width = tokens.shape
+    hidden_units = weight_out.shape[1]
+    rows = n_data * tok_count
+    own_rows = rows // 4
+    mine, part = lax.axis_index("dp"), lax.axis_index("expert")
+    high, low = part // 2, part % 2
+    in_slab = weight_in[0]
+    out_slab = weight_out[0]
+    score_total = jnp.sum(scores, axis=1, keepdims=True)
+    route_weights = ROUTE_SCALE * scores / score_total
+    experts = jnp.arange(n_data, dtype=jnp.int32)
+    chosen = expert_ids[:, :, None] == experts[None, None, :]
+    by_expert = jnp.sum(jnp.where(chosen, route_weights[:, :, None], 0.0), axis=1)
+    all_weights = gather_line(by_expert.T)
+    mine_weights = all_weights.reshape(n_data, n_data, tok_count)
+    mine_weights = jnp.sum(jnp.where((experts == mine)[None, :, None], mine_weights, 0.0), axis=1)
+    own_weight = mine_weights.reshape(4, own_rows)
+    own_weight = jnp.take(own_weight, part, axis=0)[:, None]
+    token_slab = gather_line(tokens)
+    grad_slab = gather_line(out_grad)
+    gate_up_own = sum_parts(
+        jnp.dot(token_slab, in_slab, preferred_element_type=jnp.float32), high, low
+    )
+    raw_own = sum_parts(
+        jnp.einsum("rd,fd->rf", grad_slab, out_slab, preferred_element_type=jnp.float32), high, low
+    )
+    gate, upward, sigma = gate_terms(gate_up_own, hidden_units)
+    hidden = gate * sigma * upward
+    hidden_all = join_parts((own_weight * hidden).astype(jnp.bfloat16), high, low)
+    gug_all = join_parts(gate_backward(own_weight * raw_own, gate, upward, sigma), high, low)
+    dot_own = jnp.sum(hidden * raw_own, axis=1)
+    dot_home = jnp.stack(from_offsets(join_parts(dot_own.reshape(-1, tok_count), high, low)))
+    offset = ((experts % 2) ^ (mine % 2)) * line + (experts // 2 - mine // 2) % line
+    at_offset = offset[:, None] == experts[None, :]
+    dot_by_expert = jnp.sum(jnp.where(at_offset[:, :, None], dot_home[None], 0.0), axis=1)
+    choice_dot = jnp.sum(jnp.where(chosen, dot_by_expert.T[:, None, :], 0.0), axis=2)
+    scores_grad = (
+        ROUTE_SCALE * choice_dot - jnp.sum(choice_dot * route_weights, axis=1, keepdims=True)
+    ) / score_total
+    out_rows = jnp.dot(hidden_all, out_slab, preferred_element_type=jnp.float32)
+    layer_out = send_home(out_rows.astype(jnp.bfloat16).reshape(n_data, tok_count, slab_width))
+    in_rows = jnp.einsum("rh,dh->rd", gug_all, in_slab, preferred_element_type=jnp.float32)
+    tokens_grad = send_home(in_rows.astype(jnp.bfloat16).reshape(n_data, tok_count, slab_width))
+    out_weight = jnp.einsum("rf,rd->fd", hidden_all, grad_slab, preferred_element_type=jnp.float32)
+    in_weight = jnp.einsum("rd,rh->dh", token_slab, gug_all, preferred_element_type=jnp.float32)
+    return (
+        layer_out,
+        tokens_grad,
+        scores_grad,
+        in_weight.astype(jnp.bfloat16)[None],
+        out_weight.astype(jnp.bfloat16)[None],
+    )
+
+
+def body(tokens, expert_ids, *rest):
+    n_data, n_part = lax.axis_size("dp"), lax.axis_size("expert")
+    dense = expert_ids.shape[1] == n_data and n_data % 4 == 0 and n_part == 4
+    return (dense_body if dense else routed_body)(tokens, expert_ids, *rest)
+
+
 def solution(mesh):
     placed = (
         P("dp", "expert"),

time: 359 us -> 351 us (0.978)
  starting transfers between devices: 10.4 us -> 130 us
  blocking collectives: 113 us -> 0 us
  matrix products: 49 us -> 26.4 us
  between operations: 13.9 us -> 1.4 us
  other arithmetic: 12.6 us -> 23 us
  waiting for transfers between devices: 154 us -> 159 us
  local copies, waits for them, and re-layouts: 4.91 us -> 9.42 us
    ppermute x0 -> x52, waiting for transfers between devices: none -> 159 us  [the longest x13 109 us: swap(): return lax.ppermute(value, axis, [(i, i ^ bit) for i in range(size)])]
    ppermute x0 -> x52, starting transfers between devices: none -> 130 us  [the longest x21 66.9 us: from_offsets(): arrived.append(lax.ppermute(blocks[r], 'dp', pairs))]
    all_to_all x2 -> x0, blocking collectives: 107 us -> none  [the longest x1 55.3 us: body(): lax.all_to_all(grad_send.reshape(n_data, capacity, slab_width), 'dp', spl...]
    reduce_scatter x2 -> x0, waiting for transfers between devices: 70.8 us -> none  [the longest x1 70.8 us: body(): lax.psum_scatter(jnp.dot(token_slab, in_slab, preferred_element_type=jnp....]
    all_gather x2 -> x0, waiting for transfers between devices: 47.2 us -> none  [the longest x1 25.8 us: body(): piece = lax.all_gather(gate_up_grad, 'expert', axis=0, tiled=True)]
    all_to_all x2 -> x0, waiting for transfers between devices: 36.4 us -> none  [the longest x1 22.8 us: body(): lax.all_to_all(grad_blocks, 'dp', split_axis=0, concat_axis=0, tiled=True)]
    dot_general x10 -> x6, matrix products: 49 us -> 26.4 us  [the longest x1 6.92 us: dense_body(): jnp.dot(token_slab, in_slab, preferred_element_type=jnp.float32)]
    all_to_all x2 -> x0, starting transfers between devices: 10.1 us -> none  [the longest x1 5.51 us: body(): lax.all_to_all(out_blocks, 'dp', split_axis=0, concat_axis=0, tiled=True)]
  transfers between devices with their start and end apart: 6 -> 52, of which waited for: 5 -> 22; matrix products, arithmetic and copies ran while one was open for 12% -> 11% of each run, Pallas kernels for 0% -> 0%
where the time goes in v1:
time: 351 us; the launch traced here: 349 us
  waiting for transfers between devices  159 us (45%)
  starting transfers between devices  130 us (37%)
  matrix products  26.4 us (8%)
  other arithmetic  23 us (7%)
  local copies, waits for them, and re-layouts  9.42 us (3%)
    ppermute x13, waiting for transfers between devices, swap(): return lax.ppermute(value, axis, [(i, i ^ bit) for i in range(size)])  109 us
    ppermute x21, starting transfers between devices, from_offsets(): arrived.append(lax.ppermute(blocks[r], 'dp', pairs))  66.9 us
    ppermute x9, starting transfers between devices, gather_line(): lax.ppermute(ahead[-1], 'dp', [(i, i + 2) for i in range(size - 2)])  42.4 us
    ppermute x21, waiting for transfers between devices, from_offsets(): arrived.append(lax.ppermute(blocks[r], 'dp', pairs))  23.6 us
    ppermute x9, waiting for transfers between devices, gather_line(): lax.ppermute(behind[-1], 'dp', [(i, i - 2) for i in range(2, size)])  22.1 us
    ppermute x9, starting transfers between devices, gather_line(): lax.ppermute(behind[-1], 'dp', [(i, i - 2) for i in range(2, size)])  11.7 us
    ppermute x13, starting transfers between devices, swap(): return lax.ppermute(value, axis, [(i, i ^ bit) for i in range(size)])  8.94 us
    add x2, other arithmetic, sum_parts(): pair = kept + swap(given, 'expert', 1)  8.45 us
  transfers between devices with their start and end apart: 52, of which 22 were waited for; matrix products, arithmetic and copies ran while one was open for 11% of the time, Pallas kernels for 0%

profile of v1, /device:TPU:0, one launch (start us, length us, event | category | flops | bytes accessed | tf_op | source)
XLA Modules:
  0.0 349.2 jit_solution(897022634559290852)
XLA Ops:
  2.1 5.6 %collective-permute-start.7 = (bf16[128,1024]{1,0:T(8,128)(2,1)}, bf16[128,1024]{1,0:T(8,128)(2,1)S(1)}, u32[]{:S(2)}, u32[]{:S(2)}) collective-permute-start(bf16[128,1024]{1,0:T(8,128)(2,1)} %param.6), channel_id=1, source_target_pairs={{0,8},{4,12},{8,16},{12,20},{16,24},{20,28},{1,9},{5,13},{9,17},{1... | collective-permute-start | bytes 786440 | tf_op jit(solution)/shard_map/ppermute | solution.py:143
  7.7 4.6 %collective-permute-done.8 = bf16[128,1024]{1,0:T(8,128)(2,1)S(1)} collective-permute-done((bf16[128,1024]{1,0:T(8,128)(2,1)}, bf16[128,1024]{1,0:T(8,128)(2,1)S(1)}, u32[]{:S(2)}, u32[]{:S(2)}) %collective-permute-start.8) | collective-permute-done | bytes 262176 | tf_op jit(solution)/shard_map/ppermute | solution.py:144
  13.5 4.6 %collective-permute-start.11 = (bf16[128,1024]{1,0:T(8,128)(2,1)S(1)}, bf16[128,1024]{1,0:T(8,128)(2,1)S(1)}, u32[]{:S(2)}, u32[]{:S(2)}) collective-permute-start(bf16[128,1024]{1,0:T(8,128)(2,1)S(1)} %collective-permute-done.7), channel_id=1, source_target_pairs={{0,8},{4,12},{8,16},{12,20},{16,24},{20,28},{1,9},{5,13},{9,17},{1... | collective-permute-start | bytes 786440 | tf_op jit(solution)/shard_map/ppermute | solution.py:143
  18.1 3.5 %collective-permute-done.9 = bf16[128,1024]{1,0:T(8,128)(2,1)S(1)} collective-permute-done((bf16[128,1024]{1,0:T(8,128)(2,1)S(1)}, bf16[128,1024]{1,0:T(8,128)(2,1)S(1)}, u32[]{:S(2)}, u32[]{:S(2)}) %collective-permute-start.9) | collective-permute-done | bytes 262176 | tf_op jit(solution)/shard_map/ppermute | solution.py:144
  23.9 4.6 %collective-permute-start.12 = (bf16[128,1024]{1,0:T(8,128)(2,1)S(1)}, bf16[128,1024]{1,0:T(8,128)(2,1)S(1)}, u32[]{:S(2)}, u32[]{:S(2)}) collective-permute-start(bf16[128,1024]{1,0:T(8,128)(2,1)S(1)} %collective-permute-done.11), channel_id=1, source_target_pairs={{0,8},{4,12},{8,16},{12,20},{16,24},{20,28},{1,9},{5,13},{9,17},{1... | collective-permute-start | bytes 786440 | tf_op jit(solution)/shard_map/ppermute | solution.py:143
  35.2 21.1 %collective-permute-done.13 = bf16[512,1024]{1,0:T(8,128)(2,1)} collective-permute-done((bf16[512,1024]{1,0:T(8,128)(2,1)S(1)}, bf16[512,1024]{1,0:T(8,128)(2,1)}, u32[]{:S(2)}, u32[]{:S(2)}) %collective-permute-start.13) | collective-permute-done | bytes 1048608 | tf_op jit(solution)/shard_map/ppermute | solution.py:135
  58.6 6.9 %fusion.2 = f32[2,2,256,2048]{3,2,1,0:T(8,128)S(1)} fusion(bf16[2,2,256,1024]{3,2,1,0:T(8,128)(2,1)} %bitcast.132, bf16[1,1024,2048]{2,1,0:T(8,128)(2,1)} %param.9), kind=kOutput, calls=%fused_computation.4 | convolution fusion | flops 4294967296 | bytes 14680064 | tf_op jit(solution)/shard_map/dot_general | solution.py:213
  71.4 4.7 %collective-permute-start.25 = (bf16[128,1024]{1,0:T(8,128)(2,1)S(1)}, bf16[128,1024]{1,0:T(8,128)(2,1)S(1)}, u32[]{:S(2)}, u32[]{:S(2)}) collective-permute-start(bf16[128,1024]{1,0:T(8,128)(2,1)S(1)} %copy-done.7), channel_id=1, source_target_pairs={{0,8},{4,12},{8,16},{12,20},{16,24},{20,28},{1,9},{5,13},{9,17},{1... | collective-permute-start | bytes 786440 | tf_op jit(solution)/shard_map/ppermute | solution.py:143
  76.1 5.0 %collective-permute-done.26 = bf16[128,1024]{1,0:T(8,128)(2,1)S(1)} collective-permute-done((bf16[128,1024]{1,0:T(8,128)(2,1)S(1)}, bf16[128,1024]{1,0:T(8,128)(2,1)S(1)}, u32[]{:S(2)}, u32[]{:S(2)}) %collective-permute-start.26) | collective-permute-done | bytes 262176 | tf_op jit(solution)/shard_map/ppermute | solution.py:144
  82.5 4.6 %collective-permute-start.29 = (bf16[128,1024]{1,0:T(8,128)(2,1)S(1)}, bf16[128,1024]{1,0:T(8,128)(2,1)S(1)}, u32[]{:S(2)}, u32[]{:S(2)}) collective-permute-start(bf16[128,1024]{1,0:T(8,128)(2,1)S(1)} %collective-permute-done.25), channel_id=1, source_target_pairs={{0,8},{4,12},{8,16},{12,20},{16,24},{20,28},{1,9},{5,13},{9,17},{1... | collective-permute-start | bytes 786440 | tf_op jit(solution)/shard_map/ppermute | solution.py:143
  87.0 4.2 %collective-permute-done.27 = bf16[128,1024]{1,0:T(8,128)(2,1)S(1)} collective-permute-done((bf16[128,1024]{1,0:T(8,128)(2,1)S(1)}, bf16[128,1024]{1,0:T(8,128)(2,1)S(1)}, u32[]{:S(2)}, u32[]{:S(2)}) %collective-permute-start.27) | collective-permute-done | bytes 262176 | tf_op jit(solution)/shard_map/ppermute | solution.py:144
  92.5 4.6 %collective-permute-start.30 = (bf16[128,1024]{1,0:T(8,128)(2,1)S(1)}, bf16[128,1024]{1,0:T(8,128)(2,1)S(1)}, u32[]{:S(2)}, u32[]{:S(2)}) collective-permute-start(bf16[128,1024]{1,0:T(8,128)(2,1)S(1)} %collective-permute-done.29), channel_id=1, source_target_pairs={{0,8},{4,12},{8,16},{12,20},{16,24},{20,28},{1,9},{5,13},{9,17},{1... | collective-permute-start | bytes 786440 | tf_op jit(solution)/shard_map/ppermute | solution.py:143
  102.9 21.8 %collective-permute-done.31 = bf16[512,1024]{1,0:T(8,128)(2,1)S(1)} collective-permute-done((bf16[512,1024]{1,0:T(8,128)(2,1)S(1)}, bf16[512,1024]{1,0:T(8,128)(2,1)S(1)}, u32[]{:S(2)}, u32[]{:S(2)}) %collective-permute-start.31) | collective-permute-done | bytes 1048608 | tf_op jit(solution)/shard_map/ppermute | solution.py:135
  129.8 6.1 %fusion.1 = f32[2,256,2048]{2,1,0:T(8,128)S(1)} fusion(f32[2,256,2048]{2,1,0:T(8,128)} %collective-permute-done.14, f32[2,2,256,2048]{3,2,1,0:T(8,128)} %copy-done.2, pred[]{:T(512)S(6)} %eq.34), kind=kLoop, calls=%fused_computation.3 | loop fusion | flops 2097152 | bytes 16777216 | tf_op jit(solution)/shard_map/add | solution.py:155
  140.7 21.4 %collective-permute-done.15 = bf16[256,2048]{1,0:T(8,128)(2,1)S(1)} collective-permute-done((bf16[256,2048]{1,0:T(8,128)(2,1)S(1)}, bf16[256,2048]{1,0:T(8,128)(2,1)S(1)}, u32[]{:S(2)}, u32[]{:S(2)}) %collective-permute-start.15) | collective-permute-done | bytes 1048608 | tf_op jit(solution)/shard_map/ppermute | solution.py:135
  162.8 10.2 %collective-permute-done.33 = bf16[256,1024]{1,0:T(8,128)(2,1)S(1)} collective-permute-done((bf16[256,1024]{1,0:T(8,128)(2,1)S(1)}, bf16[256,1024]{1,0:T(8,128)(2,1)S(1)}, u32[]{:S(2)}, u32[]{:S(2)}) %collective-permute-start.33) | collective-permute-done | bytes 524320 | tf_op jit(solution)/shard_map/ppermute | solution.py:135
  178.4 3.7 %collective-permute-start.45 = (f32[128]{0:T(128)S(1)}, f32[128]{0:T(128)S(1)}, u32[]{:S(2)}, u32[]{:S(2)}) collective-permute-start(f32[128]{0:T(128)S(1)} %get-tuple-element.69), channel_id=1, source_target_pairs={{0,24},{4,28},{8,0},{12,4},{16,8},{20,12},{24,16},{28,20},{1,25},{... | collective-permute-start | bytes 1544 | tf_op jit(solution)/shard_map/ppermute | solution.py:178
  189.7 3.4 collective-permute-done.50
  197.3 4.7 %collective-permute-start = (f32[8,128]{1,0:T(8,128)S(1)}, f32[8,128]{1,0:T(8,128)S(1)}, u32[]{:S(2)}, u32[]{:S(2)}) collective-permute-start(f32[8,128]{1,0:T(8,128)S(1)} %bitcast.130), channel_id=1, source_target_pairs={{0,8},{4,12},{8,16},{12,20},{16,24},{20,28},{1,9},{5,13},{9,17},{1... | collective-permute-start | bytes 12296 | tf_op jit(solution)/shard_map/ppermute | solution.py:143
  203.3 4.5 %collective-permute-start.4 = (f32[8,128]{1,0:T(8,128)S(1)}, f32[8,128]{1,0:T(8,128)S(1)}, u32[]{:S(2)}, u32[]{:S(2)}) collective-permute-start(f32[8,128]{1,0:T(8,128)S(1)} %collective-permute-done), channel_id=1, source_target_pairs={{0,8},{4,12},{8,16},{12,20},{16,24},{20,28},{1,9},{5,13},{9,17},{1... | collective-permute-start | bytes 12296 | tf_op jit(solution)/shard_map/ppermute | solution.py:143
  209.2 4.5 %collective-permute-start.5 = (f32[8,128]{1,0:T(8,128)S(1)}, f32[8,128]{1,0:T(8,128)S(1)}, u32[]{:S(2)}, u32[]{:S(2)}) collective-permute-start(f32[8,128]{1,0:T(8,128)S(1)} %collective-permute-done.4), channel_id=1, source_target_pairs={{0,8},{4,12},{8,16},{12,20},{16,24},{20,28},{1,9},{5,13},{9,17},{1... | collective-permute-start | bytes 12296 | tf_op jit(solution)/shard_map/ppermute | solution.py:143
  223.5 12.7 %collective-permute-done.16 = bf16[256,1024]{1,0:T(8,128)(2,1)S(1)} collective-permute-done((bf16[256,1024]{1,0:T(8,128)(2,1)S(1)}, bf16[256,1024]{1,0:T(8,128)(2,1)S(1)}, u32[]{:S(2)}, u32[]{:S(2)}) %collective-permute-start.16) | collective-permute-done | bytes 524320 | tf_op jit(solution)/shard_map/ppermute | solution.py:135
  236.5 15.1 %collective-permute-done.34 = bf16[256,2048]{1,0:T(8,128)(2,1)S(1)} collective-permute-done((bf16[256,2048]{1,0:T(8,128)(2,1)S(1)}, bf16[256,2048]{1,0:T(8,128)(2,1)S(1)}, u32[]{:S(2)}, u32[]{:S(2)}) %collective-permute-start.34) | collective-permute-done | bytes 1048608 | tf_op jit(solution)/shard_map/ppermute | solution.py:135
  263.1 3.8 %convert_bitcast_fusion.1 = bf16[1,1024,1024]{2,1,0:T(8,128)(2,1)} fusion(bf16[1024,1024]{1,0:T(8,128)(2,1)S(1)} %bitcast.128, bf16[1024,1024]{1,0:T(8,128)(2,1)S(1)} %copy-done.12), kind=kOutput, calls=%fused_computation.19 | convolution fusion | flops 2148532224 | bytes 6291456 | tf_op jit(solution)/shard_map/rf,rd->fd/dot_general | solution.py:235
  269.7 4.7 %fusion.14 = bf16[1024,1024]{1,0:T(8,128)(2,1)S(1)} fusion(bf16[1024,2048]{1,0:T(8,128)(2,1)S(1)} %bitcast.125, bf16[1,1024,2048]{2,1,0:T(8,128)(2,1)S(1)} %copy-done.14), kind=kOutput, calls=%fused_computation.25 | convolution fusion | flops 4296015872 | bytes 10485760 | tf_op jit(solution)/shard_map/rh,dh->rd/dot_general | solution.py:233
  278.9 6.8 %collective-permute-start.18 = (bf16[128,1024]{1,0:T(8,128)(2,1)S(1)}, bf16[128,1024]{1,0:T(8,128)(2,1)S(1)}, u32[]{:S(2)}, u32[]{:S(2)}) collective-permute-start(bf16[128,1024]{1,0:T(8,128)(2,1)S(1)} %get-tuple-element.52), channel_id=1, source_target_pairs={{0,24},{4,28},{8,0},{12,4},{16,8},{20,12},{24,16},{28,20},{1,25},{... | collective-permute-start | bytes 786440 | tf_op jit(solution)/shard_map/ppermute | solution.py:178
  285.8 10.4 %collective-permute-start.42 = (bf16[128,1024]{1,0:T(8,128)(2,1)S(1)}, bf16[128,1024]{1,0:T(8,128)(2,1)S(1)}, u32[]{:S(2)}, u32[]{:S(2)}) collective-permute-start(bf16[128,1024]{1,0:T(8,128)(2,1)S(1)} %get-tuple-element.44), channel_id=1, source_target_pairs={{0,12},{4,8},{8,20},{12,16},{16,28},{20,24},{24,4},{28,0},{1,13},{... | collective-permute-start | bytes 786440 | tf_op jit(solution)/shard_map/ppermute | solution.py:178
  296.2 15.4 %collective-permute-done.19 = bf16[128,1024]{1,0:T(8,128)(2,1)S(1)} collective-permute-done((bf16[128,1024]{1,0:T(8,128)(2,1)S(1)}, bf16[128,1024]{1,0:T(8,128)(2,1)S(1)}, u32[]{:S(2)}, u32[]{:S(2)}) %collective-permute-start.19) | collective-permute-done | bytes 262176 | tf_op jit(solution)/shard_map/ppermute | solution.py:178
  314.2 6.2 %collective-permute-start.38 = (bf16[128,1024]{1,0:T(8,128)(2,1)S(1)}, bf16[128,1024]{1,0:T(8,128)(2,1)S(1)}, u32[]{:S(2)}, u32[]{:S(2)}) collective-permute-start(bf16[128,1024]{1,0:T(8,128)(2,1)S(1)} %get-tuple-element.48), channel_id=1, source_target_pairs={{0,8},{4,12},{8,16},{12,20},{16,24},{20,28},{24,0},{28,4},{1,9},{5... | collective-permute-start | bytes 786440 | tf_op jit(solution)/shard_map/ppermute | solution.py:178
  320.4 4.4 %collective-permute-start.37 = (bf16[128,1024]{1,0:T(8,128)(2,1)S(1)}, bf16[128,1024]{1,0:T(8,128)(2,1)S(1)}, u32[]{:S(2)}, u32[]{:S(2)}) collective-permute-start(bf16[128,1024]{1,0:T(8,128)(2,1)S(1)} %get-tuple-element.49), channel_id=1, source_target_pairs={{0,16},{4,20},{8,24},{12,28},{16,0},{20,4},{24,8},{28,12},{1,17},{... | collective-permute-start | bytes 786440 | tf_op jit(solution)/shard_map/ppermute | solution.py:178
  324.8 17.1 %collective-permute-start.36 = (bf16[128,1024]{1,0:T(8,128)(2,1)S(1)}, bf16[128,1024]{1,0:T(8,128)(2,1)S(1)}, u32[]{:S(2)}, u32[]{:S(2)}) collective-permute-start(bf16[128,1024]{1,0:T(8,128)(2,1)S(1)} %get-tuple-element.43), channel_id=1, source_target_pairs={{0,24},{4,28},{8,0},{12,4},{16,8},{20,12},{24,16},{28,20},{1,25},{... | collective-permute-start | bytes 786440 | tf_op jit(solution)/shard_map/ppermute | solution.py:178
  341.9 6.2 %convert_bitcast_fusion = bf16[1,1024,2048]{2,1,0:T(8,128)(2,1)} fusion(bf16[1024,1024]{1,0:T(8,128)(2,1)S(1)} %copy-done.10, bf16[1024,2048]{1,0:T(8,128)(2,1)S(1)} %bitcast.126), kind=kOutput, calls=%fused_computation.8 | convolution fusion | flops 4297064448 | bytes 10485760 | tf_op jit(solution)/shard_map/rd,rh->dh/dot_general | solution.py:236
  (168 shorter events, 90.9 us)
Async XLA Ops:
  0.7 11.6 %collective-permute-start.8 = (bf16[128,1024]{1,0:T(8,128)(2,1)}, bf16[128,1024]{1,0:T(8,128)(2,1)S(1)}, u32[]{:S(2)}, u32[]{:S(2)}) collective-permute-start(bf16[128,1024]{1,0:T(8,128)(2,1)} %param.6), channel_id=1, source_target_pairs={{8,0},{12,4},{16,8},{20,12},{24,16},{28,20},{9,1},{13,5},{17,9},{2... | collective-permute-start | bytes 786440 | tf_op jit(solution)/shard_map/ppermute | solution.py:144
  2.1 11.4 %collective-permute-start.7 = (bf16[128,1024]{1,0:T(8,128)(2,1)}, bf16[128,1024]{1,0:T(8,128)(2,1)S(1)}, u32[]{:S(2)}, u32[]{:S(2)}) collective-permute-start(bf16[128,1024]{1,0:T(8,128)(2,1)} %param.6), channel_id=1, source_target_pairs={{0,8},{4,12},{8,16},{12,20},{16,24},{20,28},{1,9},{5,13},{9,17},{1... | collective-permute-start | bytes 786440 | tf_op jit(solution)/shard_map/ppermute | solution.py:143
  12.2 9.4 %collective-permute-start.9 = (bf16[128,1024]{1,0:T(8,128)(2,1)S(1)}, bf16[128,1024]{1,0:T(8,128)(2,1)S(1)}, u32[]{:S(2)}, u32[]{:S(2)}) collective-permute-start(bf16[128,1024]{1,0:T(8,128)(2,1)S(1)} %collective-permute-done.8), channel_id=1, source_target_pairs={{8,0},{12,4},{16,8},{20,12},{24,16},{28,20},{9,1},{13,5},{17,9},{2... | collective-permute-start | bytes 786440 | tf_op jit(solution)/shard_map/ppermute | solution.py:144
  13.5 10.3 %collective-permute-start.11 = (bf16[128,1024]{1,0:T(8,128)(2,1)S(1)}, bf16[128,1024]{1,0:T(8,128)(2,1)S(1)}, u32[]{:S(2)}, u32[]{:S(2)}) collective-permute-start(bf16[128,1024]{1,0:T(8,128)(2,1)S(1)} %collective-permute-done.7), channel_id=1, source_target_pairs={{0,8},{4,12},{8,16},{12,20},{16,24},{20,28},{1,9},{5,13},{9,17},{1... | collective-permute-start | bytes 786440 | tf_op jit(solution)/shard_map/ppermute | solution.py:143
  33.8 22.5 %collective-permute-start.13 = (bf16[512,1024]{1,0:T(8,128)(2,1)S(1)}, bf16[512,1024]{1,0:T(8,128)(2,1)}, u32[]{:S(2)}, u32[]{:S(2)}) collective-permute-start(bf16[512,1024]{1,0:T(8,128)(2,1)S(1)} %pad_maximum_fusion.3), channel_id=1, source_target_pairs={{0,4},{4,0},{8,12},{12,8},{16,20},{20,16},{24,28},{28,24},{1,5},{5... | collective-permute-start | bytes 3145736 | tf_op jit(solution)/shard_map/ppermute | solution.py:135
  70.1 59.7 %collective-permute-start.14 = (f32[2,256,2048]{2,1,0:T(8,128)}, f32[2,256,2048]{2,1,0:T(8,128)}, u32[]{:S(2)}, u32[]{:S(2)}) collective-permute-start(f32[2,256,2048]{2,1,0:T(8,128)} %select_bitcast_fusion), channel_id=1, source_target_pairs={{0,1},{1,0},{2,3},{3,2},{4,5},{5,4},{6,7},{7,6},{8,9},{9,8},{10,11... | collective-permute-start | bytes 12582920 | tf_op jit(solution)/shard_map/ppermute | solution.py:135
  70.1 11.1 %collective-permute-start.26 = (bf16[128,1024]{1,0:T(8,128)(2,1)S(1)}, bf16[128,1024]{1,0:T(8,128)(2,1)S(1)}, u32[]{:S(2)}, u32[]{:S(2)}) collective-permute-start(bf16[128,1024]{1,0:T(8,128)(2,1)S(1)} %copy-done.7), channel_id=1, source_target_pairs={{8,0},{12,4},{16,8},{20,12},{24,16},{28,20},{9,1},{13,5},{17,9},{2... | collective-permute-start | bytes 786440 | tf_op jit(solution)/shard_map/ppermute | solution.py:144
  71.4 11.1 %collective-permute-start.25 = (bf16[128,1024]{1,0:T(8,128)(2,1)S(1)}, bf16[128,1024]{1,0:T(8,128)(2,1)S(1)}, u32[]{:S(2)}, u32[]{:S(2)}) collective-permute-start(bf16[128,1024]{1,0:T(8,128)(2,1)S(1)} %copy-done.7), channel_id=1, source_target_pairs={{0,8},{4,12},{8,16},{12,20},{16,24},{20,28},{1,9},{5,13},{9,17},{1... | collective-permute-start | bytes 786440 | tf_op jit(solution)/shard_map/ppermute | solution.py:143
  81.2 10.0 %collective-permute-start.27 = (bf16[128,1024]{1,0:T(8,128)(2,1)S(1)}, bf16[128,1024]{1,0:T(8,128)(2,1)S(1)}, u32[]{:S(2)}, u32[]{:S(2)}) collective-permute-start(bf16[128,1024]{1,0:T(8,128)(2,1)S(1)} %collective-permute-done.26), channel_id=1, source_target_pairs={{8,0},{12,4},{16,8},{20,12},{24,16},{28,20},{9,1},{13,5},{17,9},{2... | collective-permute-start | bytes 786440 | tf_op jit(solution)/shard_map/ppermute | solution.py:144
  82.5 10.0 %collective-permute-start.29 = (bf16[128,1024]{1,0:T(8,128)(2,1)S(1)}, bf16[128,1024]{1,0:T(8,128)(2,1)S(1)}, u32[]{:S(2)}, u32[]{:S(2)}) collective-permute-start(bf16[128,1024]{1,0:T(8,128)(2,1)S(1)} %collective-permute-done.25), channel_id=1, source_target_pairs={{0,8},{4,12},{8,16},{12,20},{16,24},{20,28},{1,9},{5,13},{9,17},{1... | collective-permute-start | bytes 786440 | tf_op jit(solution)/shard_map/ppermute | solution.py:143
  101.7 23.0 %collective-permute-start.31 = (bf16[512,1024]{1,0:T(8,128)(2,1)S(1)}, bf16[512,1024]{1,0:T(8,128)(2,1)S(1)}, u32[]{:S(2)}, u32[]{:S(2)}) collective-permute-start(bf16[512,1024]{1,0:T(8,128)(2,1)S(1)} %pad_maximum_fusion.5), channel_id=1, source_target_pairs={{0,4},{4,0},{8,12},{12,8},{16,20},{20,16},{24,28},{28,24},{1,5},{5... | collective-permute-start | bytes 3145736 | tf_op jit(solution)/shard_map/ppermute | solution.py:135
  136.1 26.0 %collective-permute-start.15 = (bf16[256,2048]{1,0:T(8,128)(2,1)S(1)}, bf16[256,2048]{1,0:T(8,128)(2,1)S(1)}, u32[]{:S(2)}, u32[]{:S(2)}) collective-permute-start(bf16[256,2048]{1,0:T(8,128)(2,1)S(1)} %fusion.17), channel_id=1, source_target_pairs={{0,2},{1,3},{2,0},{3,1},{4,6},{5,7},{6,4},{7,5},{8,10},{9,11},{10,... | collective-permute-start | bytes 3145736 | tf_op jit(solution)/shard_map/ppermute | solution.py:135
  139.8 33.2 %collective-permute-start.33 = (bf16[256,1024]{1,0:T(8,128)(2,1)S(1)}, bf16[256,1024]{1,0:T(8,128)(2,1)S(1)}, u32[]{:S(2)}, u32[]{:S(2)}) collective-permute-start(bf16[256,1024]{1,0:T(8,128)(2,1)S(1)} %fusion.18), channel_id=1, source_target_pairs={{0,2},{1,3},{2,0},{3,1},{4,6},{5,7},{6,4},{7,5},{8,10},{9,11},{10,... | collective-permute-start | bytes 1572872 | tf_op jit(solution)/shard_map/ppermute | solution.py:135
  178.4 9.3 %collective-permute-start.45 = (f32[128]{0:T(128)S(1)}, f32[128]{0:T(128)S(1)}, u32[]{:S(2)}, u32[]{:S(2)}) collective-permute-start(f32[128]{0:T(128)S(1)} %get-tuple-element.69), channel_id=1, source_target_pairs={{0,24},{4,28},{8,0},{12,4},{16,8},{20,12},{24,16},{28,20},{1,25},{... | collective-permute-start | bytes 1544 | tf_op jit(solution)/shard_map/ppermute | solution.py:178
  221.3 14.9 %collective-permute-start.16 = (bf16[256,1024]{1,0:T(8,128)(2,1)S(1)}, bf16[256,1024]{1,0:T(8,128)(2,1)S(1)}, u32[]{:S(2)}, u32[]{:S(2)}) collective-permute-start(bf16[256,1024]{1,0:T(8,128)(2,1)S(1)} %get-tuple-element.42), channel_id=1, source_target_pairs={{0,2},{1,3},{2,0},{3,1},{4,6},{5,7},{6,4},{7,5},{8,10},{9,11},{10,... | collective-permute-start | bytes 1572872 | tf_op jit(solution)/shard_map/ppermute | solution.py:135
  223.0 28.6 %collective-permute-start.34 = (bf16[256,2048]{1,0:T(8,128)(2,1)S(1)}, bf16[256,2048]{1,0:T(8,128)(2,1)S(1)}, u32[]{:S(2)}, u32[]{:S(2)}) collective-permute-start(bf16[256,2048]{1,0:T(8,128)(2,1)S(1)} %pad_maximum_fusion.6), channel_id=1, source_target_pairs={{0,2},{1,3},{2,0},{3,1},{4,6},{5,7},{6,4},{7,5},{8,10},{9,11},{10,... | collective-permute-start | bytes 3145736 | tf_op jit(solution)/shard_map/ppermute | solution.py:135
  236.4 16.6 %collective-permute-start.17 = (bf16[2,256,1024]{2,1,0:T(8,128)(2,1)S(1)}, bf16[2,256,1024]{2,1,0:T(8,128)(2,1)S(1)}, u32[]{:S(2)}, u32[]{:S(2)}) collective-permute-start(bf16[2,256,1024]{2,1,0:T(8,128)(2,1)S(1)} %pad_maximum_fusion.4), channel_id=1, source_target_pairs={{0,1},{1,0},{2,3},{3,2},{4,5},{5,4},{6,7},{7,6},{8,9},{9,8},{10,11... | collective-permute-start | bytes 3145736 | tf_op jit(solution)/shard_map/ppermute | solution.py:135
  252.3 14.5 %collective-permute-start.35 = (bf16[2,256,2048]{2,1,0:T(8,128)(2,1)S(1)}, bf16[2,256,2048]{2,1,0:T(8,128)(2,1)S(1)}, u32[]{:S(2)}, u32[]{:S(2)}) collective-permute-start(bf16[2,256,2048]{2,1,0:T(8,128)(2,1)S(1)} %pad_maximum_fusion.2), channel_id=1, source_target_pairs={{0,1},{1,0},{2,3},{3,2},{4,5},{5,4},{6,7},{7,6},{8,9},{9,8},{10,11... | collective-permute-start | bytes 6291464 | tf_op jit(solution)/shard_map/ppermute | solution.py:135
  256.0 18.4 %collective-permute-start.24 = (bf16[128,1024]{1,0:T(8,128)(2,1)S(1)}, bf16[128,1024]{1,0:T(8,128)(2,1)S(1)}, u32[]{:S(2)}, u32[]{:S(2)}) collective-permute-start(bf16[128,1024]{1,0:T(8,128)(2,1)S(1)} %get-tuple-element.53), channel_id=1, source_target_pairs={{0,12},{4,8},{8,20},{12,16},{16,28},{20,24},{24,4},{28,0},{1,13},{... | collective-permute-start | bytes 786440 | tf_op jit(solution)/shard_map/ppermute | solution.py:178
  258.0 20.8 %collective-permute-start.23 = (bf16[128,1024]{1,0:T(8,128)(2,1)S(1)}, bf16[128,1024]{1,0:T(8,128)(2,1)S(1)}, u32[]{:S(2)}, u32[]{:S(2)}) collective-permute-start(bf16[128,1024]{1,0:T(8,128)(2,1)S(1)} %get-tuple-element.54), channel_id=1, source_target_pairs={{0,20},{4,16},{8,28},{12,24},{16,4},{20,0},{24,12},{28,8},{1,21},{... | collective-permute-start | bytes 786440 | tf_op jit(solution)/shard_map/ppermute | solution.py:178
  259.2 26.6 %collective-permute-start.22 = (bf16[128,1024]{1,0:T(8,128)(2,1)S(1)}, bf16[128,1024]{1,0:T(8,128)(2,1)S(1)}, u32[]{:S(2)}, u32[]{:S(2)}) collective-permute-start(bf16[128,1024]{1,0:T(8,128)(2,1)S(1)} %get-tuple-element.55), channel_id=1, source_target_pairs={{0,28},{4,24},{8,4},{12,0},{16,12},{20,8},{24,20},{28,16},{1,29},{... | collective-permute-start | bytes 786440 | tf_op jit(solution)/shard_map/ppermute | solution.py:178
  261.6 34.6 %collective-permute-start.21 = (bf16[128,1024]{1,0:T(8,128)(2,1)S(1)}, bf16[128,1024]{1,0:T(8,128)(2,1)S(1)}, u32[]{:S(2)}, u32[]{:S(2)}) collective-permute-start(bf16[128,1024]{1,0:T(8,128)(2,1)S(1)} %get-tuple-element.56), channel_id=1, source_target_pairs={{0,4},{4,0},{8,12},{12,8},{16,20},{20,16},{24,28},{28,24},{1,5},{5... | collective-permute-start | bytes 786440 | tf_op jit(solution)/shard_map/ppermute | solution.py:178
  266.8 29.4 %collective-permute-start.20 = (bf16[128,1024]{1,0:T(8,128)(2,1)S(1)}, bf16[128,1024]{1,0:T(8,128)(2,1)S(1)}, u32[]{:S(2)}, u32[]{:S(2)}) collective-permute-start(bf16[128,1024]{1,0:T(8,128)(2,1)S(1)} %get-tuple-element.57), channel_id=1, source_target_pairs={{0,8},{4,12},{8,16},{12,20},{16,24},{20,28},{24,0},{28,4},{1,9},{5... | collective-permute-start | bytes 786440 | tf_op jit(solution)/shard_map/ppermute | solution.py:178
  274.5 37.1 %collective-permute-start.19 = (bf16[128,1024]{1,0:T(8,128)(2,1)S(1)}, bf16[128,1024]{1,0:T(8,128)(2,1)S(1)}, u32[]{:S(2)}, u32[]{:S(2)}) collective-permute-start(bf16[128,1024]{1,0:T(8,128)(2,1)S(1)} %get-tuple-element.58), channel_id=1, source_target_pairs={{0,16},{4,20},{8,24},{12,28},{16,0},{20,4},{24,8},{28,12},{1,17},{... | collective-permute-start | bytes 786440 | tf_op jit(solution)/shard_map/ppermute | solution.py:178
  278.9 32.7 %collective-permute-start.18 = (bf16[128,1024]{1,0:T(8,128)(2,1)S(1)}, bf16[128,1024]{1,0:T(8,128)(2,1)S(1)}, u32[]{:S(2)}, u32[]{:S(2)}) collective-permute-start(bf16[128,1024]{1,0:T(8,128)(2,1)S(1)} %get-tuple-element.52), channel_id=1, source_target_pairs={{0,24},{4,28},{8,0},{12,4},{16,8},{20,12},{24,16},{28,20},{1,25},{... | collective-permute-start | bytes 786440 | tf_op jit(solution)/shard_map/ppermute | solution.py:178
  285.8 34.5 %collective-permute-start.42 = (bf16[128,1024]{1,0:T(8,128)(2,1)S(1)}, bf16[128,1024]{1,0:T(8,128)(2,1)S(1)}, u32[]{:S(2)}, u32[]{:S(2)}) collective-permute-start(bf16[128,1024]{1,0:T(8,128)(2,1)S(1)} %get-tuple-element.44), channel_id=1, source_target_pairs={{0,12},{4,8},{8,20},{12,16},{16,28},{20,24},{24,4},{28,0},{1,13},{... | collective-permute-start | bytes 786440 | tf_op jit(solution)/shard_map/ppermute | solution.py:178
  296.2 28.6 %collective-permute-start.41 = (bf16[128,1024]{1,0:T(8,128)(2,1)S(1)}, bf16[128,1024]{1,0:T(8,128)(2,1)S(1)}, u32[]{:S(2)}, u32[]{:S(2)}) collective-permute-start(bf16[128,1024]{1,0:T(8,128)(2,1)S(1)} %get-tuple-element.45), channel_id=1, source_target_pairs={{0,20},{4,16},{8,28},{12,24},{16,4},{20,0},{24,12},{28,8},{1,21},{... | collective-permute-start | bytes 786440 | tf_op jit(solution)/shard_map/ppermute | solution.py:178
  312.7 35.4 %collective-permute-start.40 = (bf16[128,1024]{1,0:T(8,128)(2,1)S(1)}, bf16[128,1024]{1,0:T(8,128)(2,1)S(1)}, u32[]{:S(2)}, u32[]{:S(2)}) collective-permute-start(bf16[128,1024]{1,0:T(8,128)(2,1)S(1)} %get-tuple-element.46), channel_id=1, source_target_pairs={{0,28},{4,24},{8,4},{12,0},{16,12},{20,8},{24,20},{28,16},{1,29},{... | collective-permute-start | bytes 786440 | tf_op jit(solution)/shard_map/ppermute | solution.py:178
  312.7 35.4 %collective-permute-start.39 = (bf16[128,1024]{1,0:T(8,128)(2,1)S(1)}, bf16[128,1024]{1,0:T(8,128)(2,1)S(1)}, u32[]{:S(2)}, u32[]{:S(2)}) collective-permute-start(bf16[128,1024]{1,0:T(8,128)(2,1)S(1)} %get-tuple-element.47), channel_id=1, source_target_pairs={{0,4},{4,0},{8,12},{12,8},{16,20},{20,16},{24,28},{28,24},{1,5},{5... | collective-permute-start | bytes 786440 | tf_op jit(solution)/shard_map/ppermute | solution.py:178
  314.2 33.9 %collective-permute-start.38 = (bf16[128,1024]{1,0:T(8,128)(2,1)S(1)}, bf16[128,1024]{1,0:T(8,128)(2,1)S(1)}, u32[]{:S(2)}, u32[]{:S(2)}) collective-permute-start(bf16[128,1024]{1,0:T(8,128)(2,1)S(1)} %get-tuple-element.48), channel_id=1, source_target_pairs={{0,8},{4,12},{8,16},{12,20},{16,24},{20,28},{24,0},{28,4},{1,9},{5... | collective-permute-start | bytes 786440 | tf_op jit(solution)/shard_map/ppermute | solution.py:178
  320.4 27.7 %collective-permute-start.37 = (bf16[128,1024]{1,0:T(8,128)(2,1)S(1)}, bf16[128,1024]{1,0:T(8,128)(2,1)S(1)}, u32[]{:S(2)}, u32[]{:S(2)}) collective-permute-start(bf16[128,1024]{1,0:T(8,128)(2,1)S(1)} %get-tuple-element.49), channel_id=1, source_target_pairs={{0,16},{4,20},{8,24},{12,28},{16,0},{20,4},{24,8},{28,12},{1,17},{... | collective-permute-start | bytes 786440 | tf_op jit(solution)/shard_map/ppermute | solution.py:178
  324.8 23.3 %collective-permute-start.36 = (bf16[128,1024]{1,0:T(8,128)(2,1)S(1)}, bf16[128,1024]{1,0:T(8,128)(2,1)S(1)}, u32[]{:S(2)}, u32[]{:S(2)}) collective-permute-start(bf16[128,1024]{1,0:T(8,128)(2,1)S(1)} %get-tuple-element.43), channel_id=1, source_target_pairs={{0,24},{4,28},{8,0},{12,4},{16,8},{20,12},{24,16},{28,20},{1,25},{... | collective-permute-start | bytes 786440 | tf_op jit(solution)/shard_map/ppermute | solution.py:178
  (35 other events, 433.3 us)
